TPU v7x, 256 devices: a whole 4x4x8 slice. The times are simulated.
256 devices in a mesh: grp: 8 (over z_hi, y), dev: 32 (over x, z_lo, core).
Axes of the slice: x: 4, y: 4, z: 8 (z_hi: 2, z_lo: 4; z = z_hi * 4 + z_lo), core: 2. Of those that a mesh axis runs over, the one named last changes fastest.
Arguments:
- embeddings: bfloat16 [98304, 768], P(('grp', 'dev')), may hold values from -6 to 6
- labels: bfloat16 [98304, 896], P(('grp', 'dev')), may hold values from -6 to 6
- cluster_rows: int32 [256], P(('grp', 'dev')), may hold values from 96 to 384, as said below
Outputs:
- propagated: bfloat16 [98304, 896], P(('grp', 'dev'))
Inputs may be any that keep to these rules, and one draw needn't show every extreme that they name: `cluster_rows`: some cluster has all 384 slots filled and some has 96.
All inputs are finite; a program needn't handle non-finite values.
Results may differ from a plain program's by a relative error of at most 0.006.
Values may be sent and summed in bfloat16 or wider, within the bound.
A program may use at most 64 MiB of HBM per device.

v0:
```python
import math

import jax
import jax.numpy as jnp
from jax import lax
from jax.sharding import PartitionSpec as P

INNER = 4


sharpness = 25.0
keep_share = 0.8


def passed_along(block, axis, distance):
    devices = range(lax.axis_size(axis))
    route = [((i - distance) % len(devices), i) for i in devices]
    return lax.ppermute(block, axis, route)


def unit_rows(embeddings):
    values = embeddings.astype(jnp.float32)
    scaled = values * lax.rsqrt(jnp.mean(values * values, axis=-1, keepdims=True) + 1e-06)
    return (scaled / math.sqrt(values.shape[-1])).astype(jnp.bfloat16)


def raw_affinity(left_unit, right_unit):
    cosine = lax.dot_general(
        left_unit, right_unit, (((1,), (1,)), ((), ())), preferred_element_type=jnp.float32
    )
    return jnp.exp(sharpness * cosine)


def backward_terms(pair_tile, own_labels):
    return lax.dot_general(
        pair_tile, own_labels, (((0,), (0,)), ((), ())), preferred_element_type=jnp.float32
    )


def body(embeddings, labels, cluster_rows):
    places = lax.iota(jnp.int32, embeddings.shape[0])
    row_valid = (places < cluster_rows[0]).astype(jnp.float32)[:, None]
    unit_vectors = unit_rows(embeddings)
    seed_labels = labels * row_valid.astype(jnp.bfloat16)
    offdiag = (places[:, None] != places[None, :]).astype(jnp.float32)
    current = seed_labels
    pair_tiles = []
    for sweep_index in range(2):
        fetched = [
            passed_along((unit_vectors, current), "dev", -offset) for offset in range(1, INNER + 1)
        ]
        cross_unit, cross_labels = passed_along((unit_vectors, current), "grp", -1)
        far_labels = [received[1] for received in fetched]
        pair_tiles = [
            raw_affinity(unit_vectors, received[0]).astype(jnp.bfloat16) for received in fetched
        ]
        pair_tiles.append(raw_affinity(unit_vectors, cross_unit).astype(jnp.bfloat16))
        pair_tiles.append((raw_affinity(unit_vectors, unit_vectors) * offdiag).astype(jnp.bfloat16))
        summed = jnp.dot(pair_tiles[INNER + 1], current, preferred_element_type=jnp.float32)
        summed = summed + jnp.dot(
            pair_tiles[INNER], cross_labels, preferred_element_type=jnp.float32
        )
        summed = summed + passed_along(
            backward_terms(pair_tiles[INNER], current).astype(jnp.bfloat16), "grp", 1
        ).astype(jnp.float32)
        returned = []
        for offset in range(INNER):
            summed = summed + jnp.dot(
                pair_tiles[offset], far_labels[offset], preferred_element_type=jnp.float32
            )
            returned.append(backward_terms(pair_tiles[offset], current))
        for offset in range(1, INNER + 1):
            summed = summed + passed_along(
                returned[offset - 1].astype(jnp.bfloat16), "dev", offset
            ).astype(jnp.float32)
        factor = lax.rsqrt(jnp.mean(summed * summed, axis=-1, keepdims=True) + 1e-06)
        mixed = keep_share * summed * factor + (1.0 - keep_share) * seed_labels.astype(jnp.float32)
        current = (mixed * row_valid).astype(jnp.bfloat16)
    return current


def solution(mesh):
    placed = (P(("grp", "dev"), None), P(("grp", "dev"), None), P(("grp", "dev")))
    return jax.shard_map(
        body, mesh=mesh, in_specs=placed, out_specs=P(("grp", "dev"), None), check_vma=False
    )
```

profile of v0, /device:TPU:1, one launch (start us, length us, event | category | flops | bytes accessed | tf_op | source)
XLA Modules:
  0.0 478.8 jit_solution(7708977031807383153)
XLA Ops:
  0.0 1.3 fusion.25
  1.3 1.3 fusion.27
  2.6 6.1 %collective-permute-start.9 = (bf16[384,768]{1,0:T(8,128)(2,1)S(1)}, bf16[384,768]{1,0:T(8,128)(2,1)S(1)}, u32[]{:S(2)}, u32[]{:S(2)}) collective-permute-start(bf16[384,768]{1,0:T(8,128)(2,1)S(1)} %fusion.27), channel_id=1, source_target_pairs={{4,0},{5,1},{6,2},{7,3},{8,4},{9,5},{10,6},{11,7},{12,8},{13,9},{1... | collective-permute-start | bytes 1769480 | tf_op jit(solution)/shard_map/ppermute | solution.py:18
  8.6 2.0 collective-permute-start.7
  10.7 2.7 collective-permute-start.3
  13.3 6.7 %collective-permute-start = (bf16[384,768]{1,0:T(8,128)(2,1)S(1)}, bf16[384,768]{1,0:T(8,128)(2,1)S(1)}, u32[]{:S(2)}, u32[]{:S(2)}) collective-permute-start(bf16[384,768]{1,0:T(8,128)(2,1)S(1)} %fusion.27), channel_id=1, source_target_pairs={{32,0},{64,32},{96,64},{128,96},{160,128},{192,160},{224,192},{0,2... | collective-permute-start | bytes 1769480 | tf_op jit(solution)/shard_map/ppermute | solution.py:18
  20.0 0.5 fusion.24
  21.1 0.1 broadcast_multiply_fusion
  21.3 0.5 fusion.30
  21.9 16.0 %collective-permute-done.9 = bf16[384,768]{1,0:T(8,128)(2,1)S(1)} collective-permute-done((bf16[384,768]{1,0:T(8,128)(2,1)S(1)}, bf16[384,768]{1,0:T(8,128)(2,1)S(1)}, u32[]{:S(2)}, u32[]{:S(2)}) %collective-permute-start.9) | collective-permute-done | bytes 589856 | tf_op jit(solution)/shard_map/ppermute | solution.py:18
  37.8 2.1 collective-permute-start.10
  40.0 0.5 fusion.19
  40.5 25.4 %collective-permute-done.7 = bf16[384,768]{1,0:T(8,128)(2,1)S(1)} collective-permute-done((bf16[384,768]{1,0:T(8,128)(2,1)S(1)}, bf16[384,768]{1,0:T(8,128)(2,1)S(1)}, u32[]{:S(2)}, u32[]{:S(2)}) %collective-permute-start.7) | collective-permute-done | bytes 589856 | tf_op jit(solution)/shard_map/ppermute | solution.py:18
  65.9 54.5 %collective-permute-start.8 = (bf16[384,896]{1,0:T(8,128)(2,1)S(1)}, bf16[384,896]{1,0:T(8,128)(2,1)S(1)}, u32[]{:S(2)}, u32[]{:S(2)}) collective-permute-start(bf16[384,896]{1,0:T(8,128)(2,1)S(1)} %broadcast_multiply_fusion), channel_id=1, source_target_pairs={{3,0},{4,1},{5,2},{6,3},{7,4},{8,5},{9,6},{10,7},{11,8},{12,9},{13... | collective-permute-start | bytes 2064392 | tf_op jit(solution)/shard_map/ppermute | solution.py:18
  120.4 0.5 fusion.20
  120.9 5.9 %collective-permute-start.6 = (bf16[384,896]{1,0:T(8,128)(2,1)S(1)}, bf16[384,896]{1,0:T(8,128)(2,1)S(1)}, u32[]{:S(2)}, u32[]{:S(2)}) collective-permute-start(bf16[384,896]{1,0:T(8,128)(2,1)S(1)} %broadcast_multiply_fusion), channel_id=1, source_target_pairs={{2,0},{3,1},{4,2},{5,3},{6,4},{7,5},{8,6},{9,7},{10,8},{11,9},{12,... | collective-permute-start | bytes 2064392 | tf_op jit(solution)/shard_map/ppermute | solution.py:18
  126.8 0.5 fusion.21
  127.3 0.6 convolution_convert_fusion.5
  127.9 0.6 convolution_convert_fusion.6
  128.6 0.5 fusion.22
  129.1 0.6 convolution_convert_fusion.7
  129.7 0.6 convolution_convert_fusion.8
  130.2 0.3 collective-permute-start.1
  130.5 0.5 fusion.23
  131.0 0.6 convolution_convert_fusion.9
  131.6 1.5 collective-permute-start.2
  133.2 0.5 fusion.34
  133.7 6.8 %collective-permute-done.8 = bf16[384,896]{1,0:T(8,128)(2,1)S(1)} collective-permute-done((bf16[384,896]{1,0:T(8,128)(2,1)S(1)}, bf16[384,896]{1,0:T(8,128)(2,1)S(1)}, u32[]{:S(2)}, u32[]{:S(2)}) %collective-permute-start.8) | collective-permute-done | bytes 688160 | tf_op jit(solution)/shard_map/ppermute | solution.py:18
  140.5 68.7 %collective-permute-start.11 = (bf16[384,896]{1,0:T(8,128)(2,1)S(1)}, bf16[384,896]{1,0:T(8,128)(2,1)S(1)}, u32[]{:S(2)}, u32[]{:S(2)}) collective-permute-start(bf16[384,896]{1,0:T(8,128)(2,1)S(1)} %convolution_convert_fusion.8), channel_id=1, source_target_pairs={{31,0},{0,1},{1,2},{2,3},{3,4},{4,5},{5,6},{6,7},{7,8},{8,9},{9,10... | collective-permute-start | bytes 2064392 | tf_op jit(solution)/shard_map/ppermute | solution.py:18
  209.2 3.1 collective-permute-start.13
  212.3 0.5 fusion.33
  212.8 0.5 fusion.32
  213.4 0.5 fusion.31
  213.9 9.9 %collective-permute-done.11 = bf16[384,896]{1,0:T(8,128)(2,1)S(1)} collective-permute-done((bf16[384,896]{1,0:T(8,128)(2,1)S(1)}, bf16[384,896]{1,0:T(8,128)(2,1)S(1)}, u32[]{:S(2)}, u32[]{:S(2)}) %collective-permute-start.11) | collective-permute-done | bytes 688160 | tf_op jit(solution)/shard_map/ppermute | solution.py:18
  223.9 19.8 %collective-permute-done.12 = bf16[384,896]{1,0:T(8,128)(2,1)S(1)} collective-permute-done((bf16[384,896]{1,0:T(8,128)(2,1)S(1)}, bf16[384,896]{1,0:T(8,128)(2,1)S(1)}, u32[]{:S(2)}, u32[]{:S(2)}) %collective-permute-start.12) | collective-permute-done | bytes 688160 | tf_op jit(solution)/shard_map/ppermute | solution.py:18
  243.7 9.7 %collective-permute-done.13 = bf16[384,896]{1,0:T(8,128)(2,1)S(1)} collective-permute-done((bf16[384,896]{1,0:T(8,128)(2,1)S(1)}, bf16[384,896]{1,0:T(8,128)(2,1)S(1)}, u32[]{:S(2)}, u32[]{:S(2)}) %collective-permute-start.13) | collective-permute-done | bytes 688160 | tf_op jit(solution)/shard_map/ppermute | solution.py:18
  253.4 64.0 %collective-permute-done.14 = bf16[384,896]{1,0:T(8,128)(2,1)S(1)} collective-permute-done((bf16[384,896]{1,0:T(8,128)(2,1)S(1)}, bf16[384,896]{1,0:T(8,128)(2,1)S(1)}, u32[]{:S(2)}, u32[]{:S(2)}) %collective-permute-start.14) | collective-permute-done | bytes 688160 | tf_op jit(solution)/shard_map/ppermute | solution.py:18
  317.4 1.2 multiply_reduce_fusion.1
  318.7 0.4 multiply_convert_fusion.1
  319.1 0.6 convolution_convert_fusion
  319.6 0.6 convolution_convert_fusion.1
  320.2 0.6 convolution_convert_fusion.4
  320.8 0.1 collective-permute-start.20
  320.9 0.1 collective-permute-start.19
  321.0 0.1 collective-permute-start.18
  321.1 3.1 collective-permute-start.17
  324.2 0.6 convolution_convert_fusion.2
  324.8 0.6 convolution_convert_fusion.3
  325.4 0.5 fusion.35
  325.9 12.5 %collective-permute-done.20 = bf16[384,896]{1,0:T(8,128)(2,1)S(1)} collective-permute-done((bf16[384,896]{1,0:T(8,128)(2,1)S(1)}, bf16[384,896]{1,0:T(8,128)(2,1)S(1)}, u32[]{:S(2)}, u32[]{:S(2)}) %collective-permute-start.20) | collective-permute-done | bytes 688160 | tf_op jit(solution)/shard_map/ppermute | solution.py:18
  338.4 10.1 %collective-permute-start.15 = (bf16[384,896]{1,0:T(8,128)(2,1)S(1)}, bf16[384,896]{1,0:T(8,128)(2,1)S(1)}, u32[]{:S(2)}, u32[]{:S(2)}) collective-permute-start(bf16[384,896]{1,0:T(8,128)(2,1)S(1)} %multiply_convert_fusion.1), channel_id=1, source_target_pairs={{32,0},{64,32},{96,64},{128,96},{160,128},{192,160},{224,192},{0,2... | collective-permute-start | bytes 2064392 | tf_op jit(solution)/shard_map/ppermute | solution.py:18
  348.5 0.5 fusion.39
  349.1 44.4 %collective-permute-done.16 = bf16[384,896]{1,0:T(8,128)(2,1)S(1)} collective-permute-done((bf16[384,896]{1,0:T(8,128)(2,1)S(1)}, bf16[384,896]{1,0:T(8,128)(2,1)S(1)}, u32[]{:S(2)}, u32[]{:S(2)}) %collective-permute-start.16) | collective-permute-done | bytes 688160 | tf_op jit(solution)/shard_map/ppermute | solution.py:18
  393.5 3.6 collective-permute-start.21
  397.3 1.9 collective-permute-start.24
  399.1 0.5 fusion.38
  399.7 0.5 fusion.37
  400.2 0.5 fusion.36
  400.7 13.5 %collective-permute-done.21 = bf16[384,896]{1,0:T(8,128)(2,1)S(1)} collective-permute-done((bf16[384,896]{1,0:T(8,128)(2,1)S(1)}, bf16[384,896]{1,0:T(8,128)(2,1)S(1)}, u32[]{:S(2)}, u32[]{:S(2)}) %collective-permute-start.21) | collective-permute-done | bytes 688160 | tf_op jit(solution)/shard_map/ppermute | solution.py:18
  414.2 17.2 %collective-permute-done.22 = bf16[384,896]{1,0:T(8,128)(2,1)S(1)} collective-permute-done((bf16[384,896]{1,0:T(8,128)(2,1)S(1)}, bf16[384,896]{1,0:T(8,128)(2,1)S(1)}, u32[]{:S(2)}, u32[]{:S(2)}) %collective-permute-start.22) | collective-permute-done | bytes 688160 | tf_op jit(solution)/shard_map/ppermute | solution.py:18
  431.4 12.3 %collective-permute-done.23 = bf16[384,896]{1,0:T(8,128)(2,1)S(1)} collective-permute-done((bf16[384,896]{1,0:T(8,128)(2,1)S(1)}, bf16[384,896]{1,0:T(8,128)(2,1)S(1)}, u32[]{:S(2)}, u32[]{:S(2)}) %collective-permute-start.23) | collective-permute-done | bytes 688160 | tf_op jit(solution)/shard_map/ppermute | solution.py:18
  443.8 32.4 %collective-permute-done.24 = bf16[384,896]{1,0:T(8,128)(2,1)S(1)} collective-permute-done((bf16[384,896]{1,0:T(8,128)(2,1)S(1)}, bf16[384,896]{1,0:T(8,128)(2,1)S(1)}, u32[]{:S(2)}, u32[]{:S(2)}) %collective-permute-start.24) | collective-permute-done | bytes 688160 | tf_op jit(solution)/shard_map/ppermute | solution.py:18
  476.1 1.2 multiply_reduce_fusion
  477.3 1.4 multiply_convert_fusion
  (26 shorter events, 0.3 us)
Async XLA Ops:
  2.5 18.6 %copy-start = (bf16[384,896]{1,0:T(8,128)(2,1)S(1)}, bf16[384,896]{1,0:T(8,128)(2,1)}, u32[]{:S(2)}) copy-start(bf16[384,896]{1,0:T(8,128)(2,1)} %param.4) | copy-start | bytes 2064388
  2.6 35.3 %collective-permute-start.9 = (bf16[384,768]{1,0:T(8,128)(2,1)S(1)}, bf16[384,768]{1,0:T(8,128)(2,1)S(1)}, u32[]{:S(2)}, u32[]{:S(2)}) collective-permute-start(bf16[384,768]{1,0:T(8,128)(2,1)S(1)} %fusion.27), channel_id=1, source_target_pairs={{4,0},{5,1},{6,2},{7,3},{8,4},{9,5},{10,6},{11,7},{12,8},{13,9},{1... | collective-permute-start | bytes 1769480 | tf_op jit(solution)/shard_map/ppermute | solution.py:18
  8.6 57.2 %collective-permute-start.7 = (bf16[384,768]{1,0:T(8,128)(2,1)S(1)}, bf16[384,768]{1,0:T(8,128)(2,1)S(1)}, u32[]{:S(2)}, u32[]{:S(2)}) collective-permute-start(bf16[384,768]{1,0:T(8,128)(2,1)S(1)} %fusion.27), channel_id=1, source_target_pairs={{3,0},{4,1},{5,2},{6,3},{7,4},{8,5},{9,6},{10,7},{11,8},{12,9},{13... | collective-permute-start | bytes 1769480 | tf_op jit(solution)/shard_map/ppermute | solution.py:18
  10.7 110.3 %collective-permute-start.5 = (bf16[384,768]{1,0:T(8,128)(2,1)S(1)}, bf16[384,768]{1,0:T(8,128)(2,1)S(1)}, u32[]{:S(2)}, u32[]{:S(2)}) collective-permute-start(bf16[384,768]{1,0:T(8,128)(2,1)S(1)} %fusion.27), channel_id=1, source_target_pairs={{2,0},{3,1},{4,2},{5,3},{6,4},{7,5},{8,6},{9,7},{10,8},{11,9},{12,... | collective-permute-start | bytes 1769480 | tf_op jit(solution)/shard_map/ppermute | solution.py:18
  10.7 117.8 %collective-permute-start.3 = (bf16[384,768]{1,0:T(8,128)(2,1)S(1)}, bf16[384,768]{1,0:T(8,128)(2,1)S(1)}, u32[]{:S(2)}, u32[]{:S(2)}) collective-permute-start(bf16[384,768]{1,0:T(8,128)(2,1)S(1)} %fusion.27), channel_id=1, source_target_pairs={{1,0},{2,1},{3,2},{4,3},{5,4},{6,5},{7,6},{8,7},{9,8},{10,9},{11,1... | collective-permute-start | bytes 1769480 | tf_op jit(solution)/shard_map/ppermute | solution.py:18
  13.3 116.9 %collective-permute-start = (bf16[384,768]{1,0:T(8,128)(2,1)S(1)}, bf16[384,768]{1,0:T(8,128)(2,1)S(1)}, u32[]{:S(2)}, u32[]{:S(2)}) collective-permute-start(bf16[384,768]{1,0:T(8,128)(2,1)S(1)} %fusion.27), channel_id=1, source_target_pairs={{32,0},{64,32},{96,64},{128,96},{160,128},{192,160},{224,192},{0,2... | collective-permute-start | bytes 1769480 | tf_op jit(solution)/shard_map/ppermute | solution.py:18
  37.8 93.8 %collective-permute-start.10 = (bf16[384,896]{1,0:T(8,128)(2,1)S(1)}, bf16[384,896]{1,0:T(8,128)(2,1)S(1)}, u32[]{:S(2)}, u32[]{:S(2)}) collective-permute-start(bf16[384,896]{1,0:T(8,128)(2,1)S(1)} %broadcast_multiply_fusion), channel_id=1, source_target_pairs={{4,0},{5,1},{6,2},{7,3},{8,4},{9,5},{10,6},{11,7},{12,8},{13,9},{1... | collective-permute-start | bytes 2064392 | tf_op jit(solution)/shard_map/ppermute | solution.py:18
  65.9 74.6 %collective-permute-start.8 = (bf16[384,896]{1,0:T(8,128)(2,1)S(1)}, bf16[384,896]{1,0:T(8,128)(2,1)S(1)}, u32[]{:S(2)}, u32[]{:S(2)}) collective-permute-start(bf16[384,896]{1,0:T(8,128)(2,1)S(1)} %broadcast_multiply_fusion), channel_id=1, source_target_pairs={{3,0},{4,1},{5,2},{6,3},{7,4},{8,5},{9,6},{10,7},{11,8},{12,9},{13... | collective-permute-start | bytes 2064392 | tf_op jit(solution)/shard_map/ppermute | solution.py:18
  120.9 88.2 %collective-permute-start.6 = (bf16[384,896]{1,0:T(8,128)(2,1)S(1)}, bf16[384,896]{1,0:T(8,128)(2,1)S(1)}, u32[]{:S(2)}, u32[]{:S(2)}) collective-permute-start(bf16[384,896]{1,0:T(8,128)(2,1)S(1)} %broadcast_multiply_fusion), channel_id=1, source_target_pairs={{2,0},{3,1},{4,2},{5,3},{6,4},{7,5},{8,6},{9,7},{10,8},{11,9},{12,... | collective-permute-start | bytes 2064392 | tf_op jit(solution)/shard_map/ppermute | solution.py:18
  128.5 80.7 %collective-permute-start.4 = (bf16[384,896]{1,0:T(8,128)(2,1)S(1)}, bf16[384,896]{1,0:T(8,128)(2,1)S(1)}, u32[]{:S(2)}, u32[]{:S(2)}) collective-permute-start(bf16[384,896]{1,0:T(8,128)(2,1)S(1)} %broadcast_multiply_fusion), channel_id=1, source_target_pairs={{1,0},{2,1},{3,2},{4,3},{5,4},{6,5},{7,6},{8,7},{9,8},{10,9},{11,1... | collective-permute-start | bytes 2064392 | tf_op jit(solution)/shard_map/ppermute | solution.py:18
  130.2 82.0 %collective-permute-start.1 = (bf16[384,896]{1,0:T(8,128)(2,1)S(1)}, bf16[384,896]{1,0:T(8,128)(2,1)S(1)}, u32[]{:S(2)}, u32[]{:S(2)}) collective-permute-start(bf16[384,896]{1,0:T(8,128)(2,1)S(1)} %broadcast_multiply_fusion), channel_id=1, source_target_pairs={{32,0},{64,32},{96,64},{128,96},{160,128},{192,160},{224,192},{0,2... | collective-permute-start | bytes 2064392 | tf_op jit(solution)/shard_map/ppermute | solution.py:18
  131.6 82.3 %collective-permute-start.2 = (bf16[384,896]{1,0:T(8,128)(2,1)S(1)}, bf16[384,896]{1,0:T(8,128)(2,1)S(1)}, u32[]{:S(2)}, u32[]{:S(2)}) collective-permute-start(bf16[384,896]{1,0:T(8,128)(2,1)S(1)} %convolution_convert_fusion.9), channel_id=1, source_target_pairs={{224,0},{0,32},{32,64},{64,96},{96,128},{128,160},{160,192},{192,2... | collective-permute-start | bytes 2064392 | tf_op jit(solution)/shard_map/ppermute | solution.py:18
  140.5 83.4 %collective-permute-start.11 = (bf16[384,896]{1,0:T(8,128)(2,1)S(1)}, bf16[384,896]{1,0:T(8,128)(2,1)S(1)}, u32[]{:S(2)}, u32[]{:S(2)}) collective-permute-start(bf16[384,896]{1,0:T(8,128)(2,1)S(1)} %convolution_convert_fusion.8), channel_id=1, source_target_pairs={{31,0},{0,1},{1,2},{2,3},{3,4},{4,5},{5,6},{6,7},{7,8},{8,9},{9,10... | collective-permute-start | bytes 2064392 | tf_op jit(solution)/shard_map/ppermute | solution.py:18
  209.2 34.5 %collective-permute-start.12 = (bf16[384,896]{1,0:T(8,128)(2,1)S(1)}, bf16[384,896]{1,0:T(8,128)(2,1)S(1)}, u32[]{:S(2)}, u32[]{:S(2)}) collective-permute-start(bf16[384,896]{1,0:T(8,128)(2,1)S(1)} %convolution_convert_fusion.7), channel_id=1, source_target_pairs={{30,0},{31,1},{0,2},{1,3},{2,4},{3,5},{4,6},{5,7},{6,8},{7,9},{8,1... | collective-permute-start | bytes 2064392 | tf_op jit(solution)/shard_map/ppermute | solution.py:18
  209.2 44.2 %collective-permute-start.13 = (bf16[384,896]{1,0:T(8,128)(2,1)S(1)}, bf16[384,896]{1,0:T(8,128)(2,1)S(1)}, u32[]{:S(2)}, u32[]{:S(2)}) collective-permute-start(bf16[384,896]{1,0:T(8,128)(2,1)S(1)} %convolution_convert_fusion.6), channel_id=1, source_target_pairs={{29,0},{30,1},{31,2},{0,3},{1,4},{2,5},{3,6},{4,7},{5,8},{6,9},{7,... | collective-permute-start | bytes 2064392 | tf_op jit(solution)/shard_map/ppermute | solution.py:18
  212.3 105.1 %collective-permute-start.14 = (bf16[384,896]{1,0:T(8,128)(2,1)S(1)}, bf16[384,896]{1,0:T(8,128)(2,1)S(1)}, u32[]{:S(2)}, u32[]{:S(2)}) collective-permute-start(bf16[384,896]{1,0:T(8,128)(2,1)S(1)} %convolution_convert_fusion.5), channel_id=1, source_target_pairs={{28,0},{29,1},{30,2},{31,3},{0,4},{1,5},{2,6},{3,7},{4,8},{5,9},{6... | collective-permute-start | bytes 2064392 | tf_op jit(solution)/shard_map/ppermute | solution.py:18
  320.8 17.6 %collective-permute-start.20 = (bf16[384,896]{1,0:T(8,128)(2,1)S(1)}, bf16[384,896]{1,0:T(8,128)(2,1)S(1)}, u32[]{:S(2)}, u32[]{:S(2)}) collective-permute-start(bf16[384,896]{1,0:T(8,128)(2,1)S(1)} %multiply_convert_fusion.1), channel_id=1, source_target_pairs={{4,0},{5,1},{6,2},{7,3},{8,4},{9,5},{10,6},{11,7},{12,8},{13,9},{1... | collective-permute-start | bytes 2064392 | tf_op jit(solution)/shard_map/ppermute | solution.py:18
  320.9 76.3 %collective-permute-start.19 = (bf16[384,896]{1,0:T(8,128)(2,1)S(1)}, bf16[384,896]{1,0:T(8,128)(2,1)S(1)}, u32[]{:S(2)}, u32[]{:S(2)}) collective-permute-start(bf16[384,896]{1,0:T(8,128)(2,1)S(1)} %multiply_convert_fusion.1), channel_id=1, source_target_pairs={{3,0},{4,1},{5,2},{6,3},{7,4},{8,5},{9,6},{10,7},{11,8},{12,9},{13... | collective-permute-start | bytes 2064392 | tf_op jit(solution)/shard_map/ppermute | solution.py:18
  321.0 76.2 %collective-permute-start.18 = (bf16[384,896]{1,0:T(8,128)(2,1)S(1)}, bf16[384,896]{1,0:T(8,128)(2,1)S(1)}, u32[]{:S(2)}, u32[]{:S(2)}) collective-permute-start(bf16[384,896]{1,0:T(8,128)(2,1)S(1)} %multiply_convert_fusion.1), channel_id=1, source_target_pairs={{2,0},{3,1},{4,2},{5,3},{6,4},{7,5},{8,6},{9,7},{10,8},{11,9},{12,... | collective-permute-start | bytes 2064392 | tf_op jit(solution)/shard_map/ppermute | solution.py:18
  321.1 76.2 %collective-permute-start.17 = (bf16[384,896]{1,0:T(8,128)(2,1)S(1)}, bf16[384,896]{1,0:T(8,128)(2,1)S(1)}, u32[]{:S(2)}, u32[]{:S(2)}) collective-permute-start(bf16[384,896]{1,0:T(8,128)(2,1)S(1)} %multiply_convert_fusion.1), channel_id=1, source_target_pairs={{1,0},{2,1},{3,2},{4,3},{5,4},{6,5},{7,6},{8,7},{9,8},{10,9},{11,1... | collective-permute-start | bytes 2064392 | tf_op jit(solution)/shard_map/ppermute | solution.py:18
  324.2 69.3 %collective-permute-start.16 = (bf16[384,896]{1,0:T(8,128)(2,1)S(1)}, bf16[384,896]{1,0:T(8,128)(2,1)S(1)}, u32[]{:S(2)}, u32[]{:S(2)}) collective-permute-start(bf16[384,896]{1,0:T(8,128)(2,1)S(1)} %convolution_convert_fusion.4), channel_id=1, source_target_pairs={{224,0},{0,32},{32,64},{64,96},{96,128},{128,160},{160,192},{192,2... | collective-permute-start | bytes 2064392 | tf_op jit(solution)/shard_map/ppermute | solution.py:18
  338.4 137.7 %collective-permute-start.15 = (bf16[384,896]{1,0:T(8,128)(2,1)S(1)}, bf16[384,896]{1,0:T(8,128)(2,1)S(1)}, u32[]{:S(2)}, u32[]{:S(2)}) collective-permute-start(bf16[384,896]{1,0:T(8,128)(2,1)S(1)} %multiply_convert_fusion.1), channel_id=1, source_target_pairs={{32,0},{64,32},{96,64},{128,96},{160,128},{192,160},{224,192},{0,2... | collective-permute-start | bytes 2064392 | tf_op jit(solution)/shard_map/ppermute | solution.py:18
  393.5 20.7 %collective-permute-start.21 = (bf16[384,896]{1,0:T(8,128)(2,1)S(1)}, bf16[384,896]{1,0:T(8,128)(2,1)S(1)}, u32[]{:S(2)}, u32[]{:S(2)}) collective-permute-start(bf16[384,896]{1,0:T(8,128)(2,1)S(1)} %convolution_convert_fusion.3), channel_id=1, source_target_pairs={{31,0},{0,1},{1,2},{2,3},{3,4},{4,5},{5,6},{6,7},{7,8},{8,9},{9,10... | collective-permute-start | bytes 2064392 | tf_op jit(solution)/shard_map/ppermute | solution.py:18
  397.1 34.3 %collective-permute-start.22 = (bf16[384,896]{1,0:T(8,128)(2,1)S(1)}, bf16[384,896]{1,0:T(8,128)(2,1)S(1)}, u32[]{:S(2)}, u32[]{:S(2)}) collective-permute-start(bf16[384,896]{1,0:T(8,128)(2,1)S(1)} %convolution_convert_fusion.2), channel_id=1, source_target_pairs={{30,0},{31,1},{0,2},{1,3},{2,4},{3,5},{4,6},{5,7},{6,8},{7,9},{8,1... | collective-permute-start | bytes 2064392 | tf_op jit(solution)/shard_map/ppermute | solution.py:18
  397.2 46.6 %collective-permute-start.23 = (bf16[384,896]{1,0:T(8,128)(2,1)S(1)}, bf16[384,896]{1,0:T(8,128)(2,1)S(1)}, u32[]{:S(2)}, u32[]{:S(2)}) collective-permute-start(bf16[384,896]{1,0:T(8,128)(2,1)S(1)} %convolution_convert_fusion.1), channel_id=1, source_target_pairs={{29,0},{30,1},{31,2},{0,3},{1,4},{2,5},{3,6},{4,7},{5,8},{6,9},{7,... | collective-permute-start | bytes 2064392 | tf_op jit(solution)/shard_map/ppermute | solution.py:18
  397.3 78.9 %collective-permute-start.24 = (bf16[384,896]{1,0:T(8,128)(2,1)S(1)}, bf16[384,896]{1,0:T(8,128)(2,1)S(1)}, u32[]{:S(2)}, u32[]{:S(2)}) collective-permute-start(bf16[384,896]{1,0:T(8,128)(2,1)S(1)} %convolution_convert_fusion), channel_id=1, source_target_pairs={{28,0},{29,1},{30,2},{31,3},{0,4},{1,5},{2,6},{3,7},{4,8},{5,9},{6... | collective-permute-start | bytes 2064392 | tf_op jit(solution)/shard_map/ppermute | solution.py:18
where the time goes:
time: 479 us
  waiting for transfers between devices  284 us (59%)
  starting transfers between devices  173 us (36%)
  matrix products  16.5 us (3%)
    ppermute x25, waiting for transfers between devices, passed_along(): return lax.ppermute(block, axis, route)  284 us
    ppermute x25, starting transfers between devices, passed_along(): return lax.ppermute(block, axis, route)  173 us
  transfers between devices with their start and end apart: 25, of which 13 were waited for; matrix products, arithmetic and copies ran while one was open for 3% of the time, Pallas kernels for 0%

commit v1 on v0

v1 whole, which is shorter than its diff:
```python
import functools
import math

import jax
import jax.numpy as jnp
from jax import lax
from jax.experimental import pallas as pl
from jax.experimental.pallas import tpu as pltpu
from jax.sharding import PartitionSpec as P

MESH = pl.DeviceIdType.MESH
F32 = jnp.float32
BF16 = jnp.bfloat16

sharpness = 25.0
keep_share = 0.8

ROWS = 384
WIDTH = 768
CLASSES = 896
LANE = 128
UN = 6
UROWS = ROWS // UN
LN = CLASSES // LANE

OWN, OUTER, INNER2, OUTER2, INNER3, OUTER3, NEXT, PREV = range(8)
SLOTS = 8

(S_OWN, S_UP, S_DOWN, S_OUTER, S_INNER2, S_OUTER2, S_WRAP_I, S_WRAP_O, S_SIB_OWN, S_SIB_OUTER, S_PART0, S_PART1,
 S_SUM) = range(13)

T_OWN, T_SIB, T_OUT, T_OUTSIB = 0, 7, 11, 15
N_TILES = 18
OWN_SOURCES = (OWN, OUTER, INNER2, OUTER2, OUTER3, NEXT, PREV)
SIB_SOURCES = (OWN, OUTER, INNER2, None)
OUT_SOURCES = (OWN, INNER2, INNER3, OUTER3)
OUTSIB_SOURCES = (OWN, OUTER3, None)


def kernel(
    count_ref, emb_ref, lab_ref, out_ref,
    ubuf, lbuf, sibu, tiles, acc, acco, psend0, psend1, precv0, precv1, ssend, srecv,
    ssem, urecv, lrecv, sibrecv, prsem, srsem,
):
    g, d = lax.axis_index("grp"), lax.axis_index("dev")
    x, k, c = d // 8, (d // 2) % 4, d % 2
    z, y = (g // 4) * 4 + k, g % 4
    s = 1 - 2 * (k // 2)
    inner = (k == 1) | (k == 2)
    edge = (y == 0) | (y == 3)

    def at(x, y, z, c):
        x, y, z = (x + 4) % 4, (y + 4) % 4, (z + 16) % 8
        return ((z // 4) * 4 + y, x * 8 + (z % 4) * 2 + c)

    sibling = at(x, y, z, 1 - c)
    ahead = at(x, y, z + s, c)
    behind = at(x, y, z - s, c)
    up, down = at(x, y + 1, z, c), at(x, y - 1, z, c)
    right, left = at(x + s, y, z, c), at(x - s, y, z, c)
    wrap_i = at(x, 3 - y, z + s + 4, c)
    wrap_o = at(x, 3 - y, z + 2 * s + 4, c)
    wrap_slot = NEXT + y // 3
    relay = at(x, 3 - y, z + 4 + s * (2 - ((k == 1) | (k == 2)).astype(jnp.int32)), c)
    side = (c + k // 2) % 2
    sib_slot = OUTER2 + 2 * side
    outsib_slot = INNER2 + 2 * side

    barrier = pltpu.get_barrier_semaphore()

    def greet(device):
        pl.semaphore_signal(barrier, inc=1, device_id=device, device_id_type=MESH)

    for device in (sibling, ahead, behind, up, down, right, left):
        greet(device)

    @pl.when(edge)
    def _():
        greet(relay)

    @pl.when(edge & inner)
    def _():
        greet(wrap_i)
        greet(wrap_o)

    def copy(src, dst, send_sem, recv_sem, device):
        return pltpu.make_async_remote_copy(
            src_ref=src, dst_ref=dst, send_sem=send_sem, recv_sem=recv_sem, device_id=device,
            device_id_type=MESH,
        )

    def rows(slot, i):
        return ubuf.at[slot, pl.ds(pl.multiple_of(i * UROWS, UROWS), UROWS)]

    def send_u(src_slot, dst_slot, i, stream, device):
        copy(
            rows(src_slot, i), rows(dst_slot, i), ssem.at[stream, 0], urecv.at[dst_slot, i], device
        ).start()

    def send_l(src_slot, dst_slot, j, stream, device):
        copy(
            lbuf.at[src_slot, j], lbuf.at[dst_slot, j], ssem.at[stream, 1], lrecv.at[dst_slot, j],
            device,
        ).start()

    def wait_u(slot, i):
        copy(rows(slot, i), rows(slot, i), ssem.at[S_OWN, 0], urecv.at[slot, i], sibling).wait_recv()

    def wait_l(slot, j):
        copy(
            lbuf.at[slot, j], lbuf.at[slot, j], ssem.at[S_OWN, 1], lrecv.at[slot, j], sibling
        ).wait_recv()

    own_slot = INNER2 - (1 - ((k == 1) | (k == 2)).astype(jnp.int32))

    def send_own(send, i):
        send(OWN, own_slot, i, S_OWN, ahead)

        @pl.when(y < 3)
        def _():
            send(OWN, PREV, i, S_UP, up)

        @pl.when(y > 0)
        def _():
            send(OWN, NEXT, i, S_DOWN, down)

    def relay_first(send, wait, i):
        wait(OUTER, i)
        send(OUTER, OUTER2, i, S_OUTER, ahead)
        wait(INNER2, i)
        send(INNER2, INNER3, i, S_INNER2, right)

        @pl.when(edge)
        def _():
            send(INNER2, wrap_slot, i, S_WRAP_I, wrap_i)

    def relay_second(send, wait, i):
        wait(OUTER2, i)
        send(OUTER2, OUTER3, i, S_OUTER2, right)

        @pl.when(edge)
        def _():
            send(OUTER2, wrap_slot, i, S_WRAP_O, wrap_o)

    valid = (lax.broadcasted_iota(jnp.int32, (ROWS, 1), 0) < count_ref[0]).astype(F32)

    values = emb_ref[...].astype(F32)
    scaled = values * lax.rsqrt(jnp.mean(values * values, axis=-1, keepdims=True) + 1e-06)
    ubuf[OWN] = (scaled / math.sqrt(WIDTH)).astype(BF16)
    pl.semaphore_wait(barrier, 7 + jnp.where(edge, 1, 0) + jnp.where(edge & inner, 2, 0))
    copy(ubuf.at[OWN], sibu.at[0], ssem.at[S_SIB_OWN, 0], sibrecv.at[0], sibling).start()
    for i in range(2):
        send_own(send_u, i)
    for j in range(LN):
        lbuf[OWN, j] = (lab_ref[:, j * LANE : (j + 1) * LANE].astype(F32) * valid).astype(BF16)

    def wait_sib_u():
        copy(ubuf.at[OWN], sibu.at[0], ssem.at[S_SIB_OWN, 0], sibrecv.at[0], sibling).wait_recv()

    def affinity(tile, left_unit, slot):
        cosine = lax.dot_general(
            left_unit, ubuf[slot], (((1,), (1,)), ((), ())), preferred_element_type=F32
        )
        tiles[tile] = jnp.exp(sharpness * cosine).astype(BF16)

    def self_tile():
        cosine = lax.dot_general(
            ubuf[OWN], ubuf[OWN], (((1,), (1,)), ((), ())), preferred_element_type=F32
        )
        a = lax.broadcasted_iota(jnp.int32, (ROWS, ROWS), 0)
        b = lax.broadcasted_iota(jnp.int32, (ROWS, ROWS), 1)
        tiles[T_OWN] = jnp.where(a == b, 0.0, jnp.exp(sharpness * cosine)).astype(BF16)

    def product(tile, slot, j):
        return jnp.dot(tiles[tile], lbuf[slot, j], preferred_element_type=F32)

    def part(buf, j):
        return buf.at[j]

    def send_part(psend, precv, kind, j):
        copy(
            psend.at[j], precv.at[j], ssem.at[S_PART0 + kind, 0], prsem.at[kind, j], sibling
        ).start()

    def wait_part(precv, kind, j):
        copy(
            precv.at[j], precv.at[j], ssem.at[S_PART0 + kind, 0], prsem.at[kind, j], sibling
        ).wait_recv()

    def finish(w):
        total = jnp.zeros((ROWS, 1), F32)
        for j in range(LN):
            summed = acc[j]
            total = total + jnp.sum(summed * summed, axis=-1, keepdims=True)
        factor = keep_share * lax.rsqrt(total / CLASSES + 1e-06) * valid
        for j in range(LN):
            seed = lbuf[OWN, j].astype(F32)
            mixed = (acc[j] * factor + (1.0 - keep_share) * valid * seed).astype(BF16)

            @pl.when(w == 0)
            def _():
                lbuf[OWN, LN + j] = mixed

            @pl.when(w == 1)
            def _():
                out_ref[:, j * LANE : (j + 1) * LANE] = mixed

    def group_products(q):
        wait_l(NEXT, q)
        wait_l(PREV, q)

    @pl.when(inner)
    def _():
        def unit_step(i, _):
            relay_first(send_u, wait_u, i)
            copy(
                rows(OUTER, i), sibu.at[1, pl.ds(pl.multiple_of(i * UROWS, UROWS), UROWS)],
                ssem.at[S_SIB_OUTER, 0], sibrecv.at[1 + i], sibling,
            ).start()

            @pl.when(i < UN - 2)
            def _():
                send_own(send_u, i + 2)

            @pl.when(i >= UN - 2)
            def _():
                send_own(send_l, i - (UN - 2))

            @pl.when(i > 0)
            def _():
                relay_second(send_u, wait_u, i - 1)

            @pl.when(i == 2)
            def _():
                self_tile()
                wait_sib_u()
                affinity(T_SIB, sibu[0], OWN)

        lax.fori_loop(0, UN, unit_step, None)
        relay_second(send_u, wait_u, UN - 1)

        def tiles_0():
            for i in range(UN):
                copy(
                    rows(OUTER, i), sibu.at[1, pl.ds(i * UROWS, UROWS)], ssem.at[S_SIB_OUTER, 0],
                    sibrecv.at[1 + i], sibling,
                ).wait_recv()
            affinity(T_OUT, ubuf[OUTER], OWN)
            affinity(T_OUTSIB, sibu[1], OWN)
            affinity(T_OWN + 1, ubuf[OWN], OUTER)
            affinity(T_SIB + 1, sibu[0], OUTER)

        def tiles_1():
            affinity(T_OWN + 2, ubuf[OWN], INNER2)
            affinity(T_SIB + 2, sibu[0], INNER2)
            affinity(T_OUT + 1, ubuf[OUTER], INNER2)
            affinity(T_OWN + 3, ubuf[OWN], OUTER2)
            for slot in (INNER3, OUTER3):
                for i in range(UN):
                    wait_u(slot, i)

        def tiles_2():
            affinity(T_SIB + 3, sibu[0], sib_slot)
            affinity(T_OUT + 2, ubuf[OUTER], INNER3)
            affinity(T_OWN + 4, ubuf[OWN], OUTER3)
            affinity(T_OUT + 3, ubuf[OUTER], OUTER3)
            affinity(T_OUTSIB + 1, sibu[1], OUTER3)
            affinity(T_OUTSIB + 2, sibu[1], outsib_slot)
            for slot in (NEXT, PREV):
                for i in range(UN):
                    wait_u(slot, i)
            affinity(T_OWN + 5, ubuf[OWN], NEXT)
            affinity(T_OWN + 6, ubuf[OWN], PREV)

        def sweep(w, _):
            base = w * LN

            def combine(q):
                wait_part(precv1, 1, base + q)
                ssend[base + q] = (acco[q] + precv1[base + q]).astype(BF16)
                copy(
                    ssend.at[base + q], srecv.at[base + q], ssem.at[S_SUM, 0], srsem.at[base + q],
                    behind,
                ).start()
                wait_part(precv0, 0, base + q)
                acc[q] += precv0[base + q]

            def grouped(q):
                wait_l(NEXT, base + q)
                wait_l(PREV, base + q)
                acc[q] += product(T_OWN + 5, NEXT, base + q) + product(T_OWN + 6, PREV, base + q)

            def compute(q, _):
                j = base + q
                wait_l(INNER3, j)
                wait_l(OUTER3, j)
                psend1[j] = (
                    product(T_OUTSIB, OWN, j)
                    + product(T_OUTSIB + 1, OUTER3, j)
                    + product(T_OUTSIB + 2, outsib_slot, j)
                )
                send_part(psend1, precv1, 1, j)
                psend0[j] = (
                    product(T_SIB, OWN, j)
                    + product(T_SIB + 1, OUTER, j)
                    + product(T_SIB + 2, INNER2, j)
                    + product(T_SIB + 3, sib_slot, j)
                )
                send_part(psend0, precv0, 0, j)
                acco[q] = (
                    product(T_OUT, OWN, j)
                    + product(T_OUT + 1, INNER2, j)
                    + product(T_OUT + 2, INNER3, j)
                    + product(T_OUT + 3, OUTER3, j)
                )
                acc[q] = (
                    product(T_OWN, OWN, j)
                    + product(T_OWN + 1, OUTER, j)
                    + product(T_OWN + 2, INNER2, j)
                    + product(T_OWN + 3, OUTER2, j)
                    + product(T_OWN + 4, OUTER3, j)
                )

                @pl.when(q > 0)
                def _():
                    combine(q - 1)
                    grouped(q - 1)

            def step(t, _):
                @pl.when(t < LN)
                def _():
                    relay_first(send_l, wait_l, base + t)

                @pl.when(t < LN - 2)
                def _():
                    send_own(send_l, base + t + 2)

                @pl.when((t > 0) & (t <= LN))
                def _():
                    relay_second(send_l, wait_l, base + t - 1)

                first = w == 0
                pl.when(first & (t == 0))(tiles_0)
                pl.when(first & (t == 1))(tiles_1)
                pl.when(first & (t == 2))(tiles_2)
                low = t - 2 - jnp.where(first & (t >= 3) & (t <= 4), 1, 0)
                low = jnp.maximum(low, 0)
                high = t - 1 - jnp.where(first & (t >= 2) & (t <= 3), 1, 0)
                lax.fori_loop(low, jnp.maximum(high, low), compute, None)

            lax.fori_loop(0, LN + 2, step, None)
            combine(LN - 1)
            grouped(LN - 1)
            finish(w)

            @pl.when(w == 0)
            def _():
                for j in range(2):
                    send_own(send_l, LN + j)

        lax.fori_loop(0, 2, sweep, None)

    @pl.when(jnp.logical_not(inner))
    def _():
        def unit_step(i, _):
            send_own(send_u, i)

        lax.fori_loop(2, UN, unit_step, None)

        def label_step(j, _):
            send_own(send_l, j)

        lax.fori_loop(0, LN, label_step, None)
        self_tile()
        wait_sib_u()
        affinity(T_SIB, sibu[0], OWN)
        for slot in (NEXT, PREV):
            for i in range(UN):
                wait_u(slot, i)
        affinity(T_OWN + 5, ubuf[OWN], NEXT)
        affinity(T_OWN + 6, ubuf[OWN], PREV)

        def sweep(w, _):
            base = w * LN

            def near(q, _):
                j = base + q
                psend0[j] = product(T_SIB, OWN, j)
                send_part(psend0, precv0, 0, j)
                acc[q] = product(T_OWN, OWN, j)

            lax.fori_loop(0, LN, near, None)

            def far(q, _):
                j = base + q
                wait_part(precv0, 0, j)
                wait_l(NEXT, j)
                wait_l(PREV, j)
                grouped = product(T_OWN + 5, NEXT, j) + product(T_OWN + 6, PREV, j)
                copy(
                    srecv.at[j], srecv.at[j], ssem.at[S_SUM, 0], srsem.at[j], ahead
                ).wait_recv()
                acc[q] += precv0[j] + grouped + srecv[j].astype(F32)

            lax.fori_loop(0, LN, far, None)
            finish(w)

            @pl.when(w == 0)
            def _():
                lax.fori_loop(LN, 2 * LN, label_step, None)

        lax.fori_loop(0, 2, sweep, None)

    def sent(slot, stream):
        copy(
            ubuf.at[slot], ubuf.at[slot], ssem.at[stream, 0], urecv.at[slot, 0], sibling
        ).wait_send()
        copy(
            lbuf.at[slot], lbuf.at[slot], ssem.at[stream, 1], lrecv.at[slot, 0], sibling
        ).wait_send()

    sent(OWN, S_OWN)
    pl.when(y < 3)(lambda: sent(OWN, S_UP))
    pl.when(y > 0)(lambda: sent(OWN, S_DOWN))
    copy(ubuf.at[OWN], sibu.at[0], ssem.at[S_SIB_OWN, 0], sibrecv.at[0], sibling).wait_send()
    copy(psend0, precv0, ssem.at[S_PART0, 0], prsem.at[0, 0], sibling).wait_send()

    @pl.when(inner)
    def _():
        sent(OUTER, S_OUTER)
        sent(INNER2, S_INNER2)
        sent(OUTER2, S_OUTER2)
        copy(ubuf.at[OUTER], sibu.at[1], ssem.at[S_SIB_OUTER, 0], sibrecv.at[1], sibling).wait_send()
        copy(psend1, precv1, ssem.at[S_PART1, 0], prsem.at[1, 0], sibling).wait_send()
        copy(ssend, srecv, ssem.at[S_SUM, 0], srsem.at[0], behind).wait_send()

    @pl.when(edge & inner)
    def _():
        sent(INNER2, S_WRAP_I)
        sent(OUTER2, S_WRAP_O)


def body(embeddings, labels, cluster_rows):
    vmem = pl.BlockSpec(memory_space=pltpu.VMEM)
    part = pltpu.VMEM((2 * LN, ROWS, LANE), F32)
    half = pltpu.VMEM((2 * LN, ROWS, LANE), BF16)
    return pl.pallas_call(
        kernel,
        out_shape=jax.ShapeDtypeStruct((ROWS, CLASSES), BF16),
        in_specs=[pl.BlockSpec(memory_space=pltpu.SMEM), vmem, vmem],
        out_specs=vmem,
        scratch_shapes=[
            pltpu.VMEM((SLOTS, ROWS, WIDTH), BF16),
            pltpu.VMEM((SLOTS, 2 * LN, ROWS, LANE), BF16),
            pltpu.VMEM((2, ROWS, WIDTH), BF16),
            pltpu.VMEM((N_TILES, ROWS, ROWS), BF16),
            pltpu.VMEM((LN, ROWS, LANE), F32),
            pltpu.VMEM((LN, ROWS, LANE), F32),
            part, part, part, part, half, half,
            pltpu.SemaphoreType.DMA((13, 2)),
            pltpu.SemaphoreType.DMA((SLOTS, UN)),
            pltpu.SemaphoreType.DMA((SLOTS, 2 * LN)),
            pltpu.SemaphoreType.DMA((1 + UN,)),
            pltpu.SemaphoreType.DMA((2, 2 * LN)),
            pltpu.SemaphoreType.DMA((2 * LN,)),
        ],
        compiler_params=pltpu.CompilerParams(
            collective_id=0, has_side_effects=True, vmem_limit_bytes=60 * 2**20
        ),
        cost_estimate=pl.CostEstimate(
            flops=14 * 10**9, bytes_accessed=2 * 10**6, transcendentals=3 * 10**6
        ),
    )(cluster_rows, embeddings, labels)


def solution(mesh):
    placed = (P(("grp", "dev"), None), P(("grp", "dev"), None), P(("grp", "dev")))
    return jax.shard_map(
        body, mesh=mesh, in_specs=placed, out_specs=P(("grp", "dev"), None), check_vma=False
    )
```

time: 479 us -> 151 us (0.32)
  waiting for transfers between devices: 284 us -> 0 us
  starting transfers between devices: 173 us -> 0 us
  Pallas kernels: 0 us -> 147 us
  matrix products: 16.5 us -> 0 us
    ppermute x25 -> x0, waiting for transfers between devices: 284 us -> none  [passed_along(): return lax.ppermute(block, axis, route)]
    ppermute x25 -> x0, starting transfers between devices: 173 us -> none  [passed_along(): return lax.ppermute(block, axis, route)]
    pallas_call x0 -> x1, Pallas kernels: none -> 147 us  [body(): pl.pallas_call(kernel, out_shape=jax.ShapeDtypeStruct((ROWS, CLASSES), BF...]
    dot_general x28 -> x0, matrix products: 16.5 us -> none  [the longest x10 5.73 us: backward_terms(): lax.dot_general(pair_tile, own_labels, (((0,), (0,)), ((), ())), preferre...]
  transfers between devices with their start and end apart: 25 -> 0, of which waited for: 13 -> 0; matrix products, arithmetic and copies ran while one was open for 3% -> 0% of each run, Pallas kernels for 0% -> 0%
where the time goes in v1:
time: 151 us; the launch traced here: 150 us
  Pallas kernels  147 us (97%)
  local copies, waits for them, and re-layouts  2 us (1%)
    pallas_call x1, Pallas kernels, body(): pl.pallas_call(kernel, out_shape=jax.ShapeDtypeStruct((ROWS, CLASSES), BF...  147 us

profile of v1, /device:TPU:1, one launch (start us, length us, event | category | flops | bytes accessed | tf_op | source)
XLA Modules:
  0.0 150.1 jit_solution(13356506272709819890)
XLA Ops:
  0.7 147.4 %shard_map.37 = bf16[384,896]{1,0:T(8,128)(2,1)} custom-call(s32[1]{0:T(128)S(6)} %copy.5.count_ref, bf16[384,768]{1,0:T(8,128)(2,1)} %emb_ref.1, bf16[384,896]{1,0:T(8,128)(2,1)} %lab_ref.1), custom_call_target="tpu_custom_call" | custom-call | flops 14000000000 | bytes 2000000 | tf_op jit(solution)/shard_map/pallas_call | solution.py:447
  148.1 2.0 %copy.6 = bf16[384,896]{1,0:T(8,128)(2,1)} copy(bf16[384,896]{1,0:T(8,128)(2,1)} %shard_map.37) | data formatting | bytes 1376256

commit v2 on v1

--- a/solution.py
+++ b/solution.py
@@ -27,7 +27,9 @@
 SLOTS = 8
 
 (S_OWN, S_UP, S_DOWN, S_OUTER, S_INNER2, S_OUTER2, S_WRAP_I, S_WRAP_O, S_SIB_OWN, S_SIB_OUTER, S_PART0, S_PART1,
- S_SUM) = range(13)
+ S_SUM, S_ASIDE, S_ONWARD) = range(15)
+NORM_STEP = 10
+DETOUR = 6
 
 T_OWN, T_SIB, T_OUT, T_OUTSIB = 0, 7, 11, 15
 N_TILES = 18
@@ -39,8 +41,8 @@
 
 def kernel(
     count_ref, emb_ref, lab_ref, out_ref,
-    ubuf, lbuf, sibu, tiles, acc, acco, psend0, psend1, precv0, precv1, ssend, srecv,
-    ssem, urecv, lrecv, sibrecv, prsem, srsem,
+    ubuf, lbuf, sibu, tiles, acc, acco, psend0, psend1, precv0, precv1, ssend, srecv, aside, norm,
+    ssem, urecv, lrecv, sibrecv, prsem, srsem, asidesem, normrecv,
 ):
     g, d = lax.axis_index("grp"), lax.axis_index("dev")
     x, k, c = d // 8, (d // 2) % 4, d % 2
@@ -66,6 +68,11 @@
     sib_slot = OUTER2 + 2 * side
     outsib_slot = INNER2 + 2 * side
 
+    beside = at(x, 1 + y // 3, z, c)
+    served = at(x, 3 - 3 * (y // 2), z + s + 4, c)
+    served_slot = NEXT + y // 2
+    server = at(x, 1 + (3 - y) // 3, z + s + 4, c)
+
     barrier = pltpu.get_barrier_semaphore()
 
     def greet(device):
@@ -82,6 +89,11 @@
     def _():
         greet(wrap_i)
         greet(wrap_o)
+        greet(server)
+
+    @pl.when(jnp.logical_not(edge) & inner)
+    def _():
+        greet(served)
 
     def copy(src, dst, send_sem, recv_sem, device):
         return pltpu.make_async_remote_copy(
@@ -111,6 +123,16 @@
             lbuf.at[slot, j], lbuf.at[slot, j], ssem.at[S_OWN, 1], lrecv.at[slot, j], sibling
         ).wait_recv()
 
+    def send_norm(src_slot, dst_slot, _, stream, device):
+        copy(
+            norm.at[src_slot], norm.at[dst_slot], ssem.at[stream, 2], normrecv.at[dst_slot], device
+        ).start()
+
+    def wait_norm(slot, _):
+        copy(
+            norm.at[slot], norm.at[slot], ssem.at[S_OWN, 2], normrecv.at[slot], sibling
+        ).wait_recv()
+
     own_slot = INNER2 - (1 - ((k == 1) | (k == 2)).astype(jnp.int32))
 
     def send_own(send, i):
@@ -124,12 +146,15 @@
         def _():
             send(OWN, NEXT, i, S_DOWN, down)
 
-    def relay_first(send, wait, i):
+    def relay_outer(send, wait, i):
         wait(OUTER, i)
         send(OUTER, OUTER2, i, S_OUTER, ahead)
+
+    def relay_inner(send, wait, i):
         wait(INNER2, i)
         send(INNER2, INNER3, i, S_INNER2, right)
 
+    def wrap_inner(send, i):
         @pl.when(edge)
         def _():
             send(INNER2, wrap_slot, i, S_WRAP_I, wrap_i)
@@ -142,12 +167,15 @@
         def _():
             send(OUTER2, wrap_slot, i, S_WRAP_O, wrap_o)
 
+    acc[...] = jnp.zeros_like(acc)
     valid = (lax.broadcasted_iota(jnp.int32, (ROWS, 1), 0) < count_ref[0]).astype(F32)
 
     values = emb_ref[...].astype(F32)
     scaled = values * lax.rsqrt(jnp.mean(values * values, axis=-1, keepdims=True) + 1e-06)
     ubuf[OWN] = (scaled / math.sqrt(WIDTH)).astype(BF16)
-    pl.semaphore_wait(barrier, 7 + jnp.where(edge, 1, 0) + jnp.where(edge & inner, 2, 0))
+    pl.semaphore_wait(
+        barrier, 7 + jnp.where(inner, jnp.where(edge, 4, 1), jnp.where(edge, 1, 0))
+    )
     copy(ubuf.at[OWN], sibu.at[0], ssem.at[S_SIB_OWN, 0], sibrecv.at[0], sibling).start()
     for i in range(2):
         send_own(send_u, i)
@@ -167,16 +195,11 @@
         cosine = lax.dot_general(
             ubuf[OWN], ubuf[OWN], (((1,), (1,)), ((), ())), preferred_element_type=F32
         )
-        a = lax.broadcasted_iota(jnp.int32, (ROWS, ROWS), 0)
-        b = lax.broadcasted_iota(jnp.int32, (ROWS, ROWS), 1)
-        tiles[T_OWN] = jnp.where(a == b, 0.0, jnp.exp(sharpness * cosine)).astype(BF16)
+        tiles[T_OWN] = jnp.where(diagonal(), 0.0, jnp.exp(sharpness * cosine)).astype(BF16)
 
     def product(tile, slot, j):
         return jnp.dot(tiles[tile], lbuf[slot, j], preferred_element_type=F32)
 
-    def part(buf, j):
-        return buf.at[j]
-
     def send_part(psend, precv, kind, j):
         copy(
             psend.at[j], precv.at[j], ssem.at[S_PART0 + kind, 0], prsem.at[kind, j], sibling
@@ -187,32 +210,42 @@
             precv.at[j], precv.at[j], ssem.at[S_PART0 + kind, 0], prsem.at[kind, j], sibling
         ).wait_recv()
 
-    def finish(w):
+    def row_factor():
         total = jnp.zeros((ROWS, 1), F32)
         for j in range(LN):
             summed = acc[j]
             total = total + jnp.sum(summed * summed, axis=-1, keepdims=True)
-        factor = keep_share * lax.rsqrt(total / CLASSES + 1e-06) * valid
+        return keep_share * lax.rsqrt(total / CLASSES + 1e-06) * valid
+
+    def diagonal():
+        a = lax.broadcasted_iota(jnp.int32, (ROWS, ROWS), 0)
+        return a == lax.broadcasted_iota(jnp.int32, (ROWS, ROWS), 1)
+
+    def share_factor():
+        row = jnp.sum(jnp.where(diagonal(), row_factor(), 0.0), axis=0, keepdims=True)
+        norm[OWN] = jnp.broadcast_to(row, (8, ROWS))
+        send_own(send_norm, 0)
+
+    def finish():
+        factor = row_factor()
         for j in range(LN):
             seed = lbuf[OWN, j].astype(F32)
-            mixed = (acc[j] * factor + (1.0 - keep_share) * valid * seed).astype(BF16)
-
-            @pl.when(w == 0)
-            def _():
-                lbuf[OWN, LN + j] = mixed
-
-            @pl.when(w == 1)
-            def _():
-                out_ref[:, j * LANE : (j + 1) * LANE] = mixed
-
-    def group_products(q):
-        wait_l(NEXT, q)
-        wait_l(PREV, q)
+            mixed = acc[j] * factor + (1.0 - keep_share) * seed
+            out_ref[:, j * LANE : (j + 1) * LANE] = mixed.astype(BF16)
+
+    def send_sum(q):
+        lbuf[OWN, LN + q] = acc[q].astype(BF16)
+        send_own(send_l, LN + q)
+
+    def scale(tile, slot):
+        tiles[tile] = (tiles[tile].astype(F32) * norm[slot, 0:1]).astype(BF16)
 
     @pl.when(inner)
     def _():
         def unit_step(i, _):
-            relay_first(send_u, wait_u, i)
+            relay_outer(send_u, wait_u, i)
+            relay_inner(send_u, wait_u, i)
+            wrap_inner(send_u, i)
             copy(
                 rows(OUTER, i), sibu.at[1, pl.ds(pl.multiple_of(i * UROWS, UROWS), UROWS)],
                 ssem.at[S_SIB_OUTER, 0], sibrecv.at[1 + i], sibling,
@@ -272,93 +305,159 @@
             affinity(T_OWN + 5, ubuf[OWN], NEXT)
             affinity(T_OWN + 6, ubuf[OWN], PREV)
 
-        def sweep(w, _):
-            base = w * LN
-
-            def combine(q):
-                wait_part(precv1, 1, base + q)
-                ssend[base + q] = (acco[q] + precv1[base + q]).astype(BF16)
-                copy(
-                    ssend.at[base + q], srecv.at[base + q], ssem.at[S_SUM, 0], srsem.at[base + q],
-                    behind,
-                ).start()
-                wait_part(precv0, 0, base + q)
-                acc[q] += precv0[base + q]
-
-            def grouped(q):
-                wait_l(NEXT, base + q)
-                wait_l(PREV, base + q)
-                acc[q] += product(T_OWN + 5, NEXT, base + q) + product(T_OWN + 6, PREV, base + q)
-
-            def compute(q, _):
-                j = base + q
-                wait_l(INNER3, j)
-                wait_l(OUTER3, j)
-                psend1[j] = (
-                    product(T_OUTSIB, OWN, j)
-                    + product(T_OUTSIB + 1, OUTER3, j)
-                    + product(T_OUTSIB + 2, outsib_slot, j)
-                )
-                send_part(psend1, precv1, 1, j)
-                psend0[j] = (
-                    product(T_SIB, OWN, j)
-                    + product(T_SIB + 1, OUTER, j)
-                    + product(T_SIB + 2, INNER2, j)
-                    + product(T_SIB + 3, sib_slot, j)
-                )
-                send_part(psend0, precv0, 0, j)
-                acco[q] = (
-                    product(T_OUT, OWN, j)
-                    + product(T_OUT + 1, INNER2, j)
-                    + product(T_OUT + 2, INNER3, j)
-                    + product(T_OUT + 3, OUTER3, j)
-                )
-                acc[q] = (
-                    product(T_OWN, OWN, j)
-                    + product(T_OWN + 1, OUTER, j)
-                    + product(T_OWN + 2, INNER2, j)
-                    + product(T_OWN + 3, OUTER2, j)
-                    + product(T_OWN + 4, OUTER3, j)
-                )
-
-                @pl.when(q > 0)
+        def scale_near():
+            for i, slot in ((0, OWN), (1, OUTER), (2, INNER2)):
+                scale(T_OWN + i, slot)
+                scale(T_SIB + i, slot)
+            scale(T_OUT, OWN)
+            scale(T_OUT + 1, INNER2)
+            scale(T_OUTSIB, OWN)
+
+        def scale_far():
+            scale(T_OWN + 3, OUTER2)
+            scale(T_OWN + 4, OUTER3)
+            scale(T_SIB + 3, sib_slot)
+            scale(T_OUT + 2, INNER3)
+            scale(T_OUT + 3, OUTER3)
+            scale(T_OUTSIB + 1, OUTER3)
+            scale(T_OUTSIB + 2, outsib_slot)
+            scale(T_OWN + 5, NEXT)
+            scale(T_OWN + 6, PREV)
+
+        def combine(q, j):
+            wait_part(precv1, 1, j)
+            ssend[j] = (acco[q] + precv1[j]).astype(BF16)
+
+            copy(ssend.at[j], srecv.at[j], ssem.at[S_SUM, 0], srsem.at[j], behind).start()
+            wait_part(precv0, 0, j)
+            acc[q] += precv0[j]
+
+        def onward(j):
+            copy(
+                aside.at[j], aside.at[j], ssem.at[S_ASIDE, 0], asidesem.at[j], sibling
+            ).wait_recv()
+            copy(
+                aside.at[j], lbuf.at[served_slot, j], ssem.at[S_ONWARD, 0],
+                lrecv.at[served_slot, j], served,
+            ).start()
+
+        def grouped(q, j):
+            wait_l(NEXT, j)
+            wait_l(PREV, j)
+            acc[q] += product(T_OWN + 5, NEXT, j) + product(T_OWN + 6, PREV, j)
+
+        def compute(j, _):
+            second = j // LN
+            q = j - second * LN
+            kept = jnp.where(second == 0, 0.0, 1.0 - keep_share)
+            wait_l(INNER3, j)
+            wait_l(OUTER3, j)
+            psend1[j] = (
+                product(T_OUTSIB, OWN, j)
+                + product(T_OUTSIB + 1, OUTER3, j)
+                + product(T_OUTSIB + 2, outsib_slot, j)
+            )
+            send_part(psend1, precv1, 1, j)
+            psend0[j] = (
+                product(T_SIB, OWN, j)
+                + product(T_SIB + 1, OUTER, j)
+                + product(T_SIB + 2, INNER2, j)
+                + product(T_SIB + 3, sib_slot, j)
+            )
+            send_part(psend0, precv0, 0, j)
+            acco[q] = (
+                product(T_OUT, OWN, j)
+                + product(T_OUT + 1, INNER2, j)
+                + product(T_OUT + 2, INNER3, j)
+                + product(T_OUT + 3, OUTER3, j)
+            )
+            acc[q] = acc[q] * kept + (
+                product(T_OWN, OWN, j)
+                + product(T_OWN + 1, OUTER, j)
+                + product(T_OWN + 2, INNER2, j)
+                + product(T_OWN + 3, OUTER2, j)
+                + product(T_OWN + 4, OUTER3, j)
+            )
+            combine(q, j)
+
+            @pl.when(q > 1)
+            def _():
+                grouped(q - 2, j - 2)
+
+        def done(n):
+            one = jnp.where(n >= 4, n - 1, jnp.where(n == 3, 1, 0))
+            return jnp.where(n < 9, one, jnp.clip(7 + 2 * (n - 11), 7, 14))
+
+        def step(n, _):
+            @pl.when(n < 2 * LN)
+            def _():
+                relay_outer(send_l, wait_l, n)
+
+            @pl.when(n < LN - 2)
+            def _():
+                send_own(send_l, n + 2)
+
+            @pl.when((n >= LN - 2) & (n < 2 * LN - 2))
+            def _():
+                send_sum(n - (LN - 2))
+
+            @pl.when(n < 2 * LN)
+            def _():
+                relay_inner(send_l, wait_l, n)
+
+                @pl.when(n - (n // LN) * LN >= DETOUR)
                 def _():
-                    combine(q - 1)
-                    grouped(q - 1)
-
-            def step(t, _):
-                @pl.when(t < LN)
+                    wrap_inner(send_l, n)
+
+                @pl.when(edge & (n - (n // LN) * LN < DETOUR))
                 def _():
-                    relay_first(send_l, wait_l, base + t)
-
-                @pl.when(t < LN - 2)
-                def _():
-                    send_own(send_l, base + t + 2)
-
-                @pl.when((t > 0) & (t <= LN))
-                def _():
-                    relay_second(send_l, wait_l, base + t - 1)
-
-                first = w == 0
-                pl.when(first & (t == 0))(tiles_0)
-                pl.when(first & (t == 1))(tiles_1)
-                pl.when(first & (t == 2))(tiles_2)
-                low = t - 2 - jnp.where(first & (t >= 3) & (t <= 4), 1, 0)
-                low = jnp.maximum(low, 0)
-                high = t - 1 - jnp.where(first & (t >= 2) & (t <= 3), 1, 0)
-                lax.fori_loop(low, jnp.maximum(high, low), compute, None)
-
-            lax.fori_loop(0, LN + 2, step, None)
-            combine(LN - 1)
-            grouped(LN - 1)
-            finish(w)
-
-            @pl.when(w == 0)
-            def _():
-                for j in range(2):
-                    send_own(send_l, LN + j)
-
-        lax.fori_loop(0, 2, sweep, None)
+                    copy(
+                        lbuf.at[INNER2, n], aside.at[n], ssem.at[S_ASIDE, 1], asidesem.at[n],
+                        beside,
+                    ).start()
+
+            @pl.when((n > 0) & (n <= 2 * LN))
+            def _():
+                relay_second(send_l, wait_l, n - 1)
+
+            late = n - 2
+
+            @pl.when((n >= 2) & (late - (late // LN) * LN < DETOUR) & jnp.logical_not(edge))
+            def _():
+                onward(late)
+
+            pl.when(n == 0)(tiles_0)
+            pl.when(n == 1)(tiles_1)
+            pl.when(n == 2)(tiles_2)
+
+            @pl.when(n == NORM_STEP)
+            def _():
+                relay_outer(send_norm, wait_norm, 0)
+                relay_inner(send_norm, wait_norm, 0)
+                wrap_inner(send_norm, 0)
+
+            @pl.when(n == NORM_STEP + 1)
+            def _():
+                relay_second(send_norm, wait_norm, 0)
+                scale_near()
+
+            @pl.when(n == NORM_STEP + 2)
+            def _():
+                for slot in (INNER3, OUTER3, NEXT, PREV):
+                    wait_norm(slot, 0)
+                scale_far()
+
+            lax.fori_loop(jnp.where(n == 0, 0, done(n - 1)), done(n), compute, None)
+
+            @pl.when(n == LN + 1)
+            def _():
+                grouped(LN - 2, LN - 2)
+                grouped(LN - 1, LN - 1)
+                share_factor()
+
+        lax.fori_loop(0, 2 * LN + 2, step, None)
+        grouped(LN - 2, 2 * LN - 2)
+        grouped(LN - 1, 2 * LN - 1)
 
     @pl.when(jnp.logical_not(inner))
     def _():
@@ -380,36 +479,37 @@
         affinity(T_OWN + 5, ubuf[OWN], NEXT)
         affinity(T_OWN + 6, ubuf[OWN], PREV)
 
-        def sweep(w, _):
-            base = w * LN
-
-            def near(q, _):
-                j = base + q
-                psend0[j] = product(T_SIB, OWN, j)
-                send_part(psend0, precv0, 0, j)
-                acc[q] = product(T_OWN, OWN, j)
-
-            lax.fori_loop(0, LN, near, None)
-
-            def far(q, _):
-                j = base + q
-                wait_part(precv0, 0, j)
-                wait_l(NEXT, j)
-                wait_l(PREV, j)
-                grouped = product(T_OWN + 5, NEXT, j) + product(T_OWN + 6, PREV, j)
-                copy(
-                    srecv.at[j], srecv.at[j], ssem.at[S_SUM, 0], srsem.at[j], ahead
-                ).wait_recv()
-                acc[q] += precv0[j] + grouped + srecv[j].astype(F32)
-
-            lax.fori_loop(0, LN, far, None)
-            finish(w)
-
-            @pl.when(w == 0)
-            def _():
-                lax.fori_loop(LN, 2 * LN, label_step, None)
-
-        lax.fori_loop(0, 2, sweep, None)
+        def near(j, _):
+            second = j // LN
+            q = j - second * LN
+            psend0[j] = product(T_SIB, OWN, j)
+            send_part(psend0, precv0, 0, j)
+            kept = jnp.where(second == 0, 0.0, 1.0 - keep_share)
+            acc[q] = acc[q] * kept + product(T_OWN, OWN, j)
+
+        def far(j, _):
+            q = j - (j // LN) * LN
+            wait_part(precv0, 0, j)
+            wait_l(NEXT, j)
+            wait_l(PREV, j)
+            grouped = product(T_OWN + 5, NEXT, j) + product(T_OWN + 6, PREV, j)
+            copy(srecv.at[j], srecv.at[j], ssem.at[S_SUM, 0], srsem.at[j], ahead).wait_recv()
+            acc[q] += precv0[j] + grouped + srecv[j].astype(F32)
+            pl.when(j < LN)(lambda: send_sum(q))
+
+        lax.fori_loop(0, LN, near, None)
+        lax.fori_loop(0, LN, far, None)
+        share_factor()
+        scale(T_OWN, OWN)
+        scale(T_SIB, OWN)
+        lax.fori_loop(LN, 2 * LN, near, None)
+        wait_norm(NEXT, 0)
+        wait_norm(PREV, 0)
+        scale(T_OWN + 5, NEXT)
+        scale(T_OWN + 6, PREV)
+        lax.fori_loop(LN, 2 * LN, far, None)
+
+    finish()
 
     def sent(slot, stream):
         copy(
@@ -418,6 +518,7 @@
         copy(
             lbuf.at[slot], lbuf.at[slot], ssem.at[stream, 1], lrecv.at[slot, 0], sibling
         ).wait_send()
+        copy(norm.at[slot], norm.at[slot], ssem.at[stream, 2], normrecv.at[slot], sibling).wait_send()
 
     sent(OWN, S_OWN)
     pl.when(y < 3)(lambda: sent(OWN, S_UP))
@@ -432,12 +533,27 @@
         sent(OUTER2, S_OUTER2)
         copy(ubuf.at[OUTER], sibu.at[1], ssem.at[S_SIB_OUTER, 0], sibrecv.at[1], sibling).wait_send()
         copy(psend1, precv1, ssem.at[S_PART1, 0], prsem.at[1, 0], sibling).wait_send()
+
+    @pl.when(inner)
+    def _():
         copy(ssend, srecv, ssem.at[S_SUM, 0], srsem.at[0], behind).wait_send()
 
+    @pl.when(inner & jnp.logical_not(edge))
+    def _():
+        some = aside.at[pl.ds(0, 2 * DETOUR)]
+        copy(some, some, ssem.at[S_ONWARD, 0], asidesem.at[0], sibling).wait_send()
+
     @pl.when(edge & inner)
     def _():
-        sent(INNER2, S_WRAP_I)
         sent(OUTER2, S_WRAP_O)
+        block = ubuf.at[INNER2]
+        copy(block, block, ssem.at[S_WRAP_I, 0], urecv.at[INNER2, 0], sibling).wait_send()
+        some = lbuf.at[INNER2, pl.ds(0, 2 * (LN - DETOUR))]
+        copy(some, some, ssem.at[S_WRAP_I, 1], lrecv.at[INNER2, 0], sibling).wait_send()
+        row = norm.at[INNER2]
+        copy(row, row, ssem.at[S_WRAP_I, 2], normrecv.at[INNER2], sibling).wait_send()
+        some = lbuf.at[INNER2, pl.ds(0, 2 * DETOUR)]
+        copy(some, some, ssem.at[S_ASIDE, 1], lrecv.at[INNER2, 0], sibling).wait_send()
 
 
 def body(embeddings, labels, cluster_rows):
@@ -456,13 +572,16 @@
             pltpu.VMEM((N_TILES, ROWS, ROWS), BF16),
             pltpu.VMEM((LN, ROWS, LANE), F32),
             pltpu.VMEM((LN, ROWS, LANE), F32),
-            part, part, part, part, half, half,
-            pltpu.SemaphoreType.DMA((13, 2)),
+            part, part, part, part, half, half, half,
+            pltpu.VMEM((SLOTS, 8, ROWS), F32),
+            pltpu.SemaphoreType.DMA((15, 3)),
             pltpu.SemaphoreType.DMA((SLOTS, UN)),
             pltpu.SemaphoreType.DMA((SLOTS, 2 * LN)),
             pltpu.SemaphoreType.DMA((1 + UN,)),
             pltpu.SemaphoreType.DMA((2, 2 * LN)),
             pltpu.SemaphoreType.DMA((2 * LN,)),
+            pltpu.SemaphoreType.DMA((2 * LN,)),
+            pltpu.SemaphoreType.DMA((SLOTS,)),
         ],
         compiler_params=pltpu.CompilerParams(
             collective_id=0, has_side_effects=True, vmem_limit_bytes=60 * 2**20

time: 151 us -> 134 us (0.89)
  Pallas kernels: 147 us -> 131 us
    pallas_call x1, Pallas kernels: 147 us -> 131 us  [body(): pl.pallas_call(kernel, out_shape=jax.ShapeDtypeStruct((ROWS, CLASSES), BF...]
where the time goes in v2:
time: 134 us
  Pallas kernels  131 us (98%)
  local copies, waits for them, and re-layouts  2 us (1%)
    pallas_call x1, Pallas kernels, body(): pl.pallas_call(kernel, out_shape=jax.ShapeDtypeStruct((ROWS, CLASSES), BF...  131 us

profile of v2, /device:TPU:1, one launch (start us, length us, event | category | flops | bytes accessed | tf_op | source)
XLA Modules:
  0.0 134.0 jit_solution(14772044712612077012)
XLA Ops:
  0.7 131.4 %shard_map.37 = bf16[384,896]{1,0:T(8,128)(2,1)} custom-call(s32[1]{0:T(128)S(6)} %copy.5.count_ref, bf16[384,768]{1,0:T(8,128)(2,1)} %emb_ref.1, bf16[384,896]{1,0:T(8,128)(2,1)} %lab_ref.1), custom_call_target="tpu_custom_call" | custom-call | flops 14000000000 | bytes 2000000 | tf_op jit(solution)/shard_map/pallas_call | solution.py:563
  132.0 2.0 %copy.6 = bf16[384,896]{1,0:T(8,128)(2,1)} copy(bf16[384,896]{1,0:T(8,128)(2,1)} %shard_map.37) | data formatting | bytes 1376256

commit v3 on v2

--- a/solution.py
+++ b/solution.py
@@ -28,8 +28,8 @@
 
 (S_OWN, S_UP, S_DOWN, S_OUTER, S_INNER2, S_OUTER2, S_WRAP_I, S_WRAP_O, S_SIB_OWN, S_SIB_OUTER, S_PART0, S_PART1,
  S_SUM, S_ASIDE, S_ONWARD) = range(15)
-NORM_STEP = 10
-DETOUR = 6
+NORM_STEP = 9
+DETOUR = 13
 
 T_OWN, T_SIB, T_OUT, T_OUTSIB = 0, 7, 11, 15
 N_TILES = 18
@@ -41,8 +41,8 @@
 
 def kernel(
     count_ref, emb_ref, lab_ref, out_ref,
-    ubuf, lbuf, sibu, tiles, acc, acco, psend0, psend1, precv0, precv1, ssend, srecv, aside, norm,
-    ssem, urecv, lrecv, sibrecv, prsem, srsem, asidesem, normrecv,
+    ubuf, lbuf, sibu, tiles, acc, acco, psend0, psend1, precv0, precv1, ssend, srecv, aside, asideu, norm,
+    ssem, urecv, lrecv, sibrecv, prsem, srsem, asidesem, asideusem, normrecv,
 ):
     g, d = lax.axis_index("grp"), lax.axis_index("dev")
     x, k, c = d // 8, (d // 2) % 4, d % 2
@@ -242,10 +242,32 @@
 
     @pl.when(inner)
     def _():
+        def aside_rows(i):
+            return asideu.at[pl.ds(pl.multiple_of(i * UROWS, UROWS), UROWS)]
+
+        def onward_u(i):
+            copy(
+                aside_rows(i), aside_rows(i), ssem.at[S_ASIDE, 0], asideusem.at[i], sibling
+            ).wait_recv()
+            copy(
+                aside_rows(i), rows(served_slot, i), ssem.at[S_ONWARD, 1],
+                urecv.at[served_slot, i], served,
+            ).start()
+
         def unit_step(i, _):
             relay_outer(send_u, wait_u, i)
             relay_inner(send_u, wait_u, i)
-            wrap_inner(send_u, i)
+
+            @pl.when(edge)
+            def _():
+                copy(
+                    rows(INNER2, i), aside_rows(i), ssem.at[S_ASIDE, 0], asideusem.at[i], beside
+                ).start()
+
+            @pl.when((i >= 2) & jnp.logical_not(edge))
+            def _():
+                onward_u(i - 2)
+
             copy(
                 rows(OUTER, i), sibu.at[1, pl.ds(pl.multiple_of(i * UROWS, UROWS), UROWS)],
                 ssem.at[S_SIB_OUTER, 0], sibrecv.at[1 + i], sibling,
@@ -299,6 +321,8 @@
             affinity(T_OUT + 3, ubuf[OUTER], OUTER3)
             affinity(T_OUTSIB + 1, sibu[1], OUTER3)
             affinity(T_OUTSIB + 2, sibu[1], outsib_slot)
+
+        def tiles_3():
             for slot in (NEXT, PREV):
                 for i in range(UN):
                     wait_u(slot, i)
@@ -378,7 +402,13 @@
                 + product(T_OWN + 3, OUTER2, j)
                 + product(T_OWN + 4, OUTER3, j)
             )
-            combine(q, j)
+            @pl.when(q > 0)
+            def _():
+                combine(q - 1, j - 1)
+
+            @pl.when(q == LN - 1)
+            def _():
+                combine(q, j)
 
             @pl.when(q > 1)
             def _():
@@ -405,11 +435,11 @@
             def _():
                 relay_inner(send_l, wait_l, n)
 
-                @pl.when(n - (n // LN) * LN >= DETOUR)
+                @pl.when(n >= DETOUR)
                 def _():
                     wrap_inner(send_l, n)
 
-                @pl.when(edge & (n - (n // LN) * LN < DETOUR))
+                @pl.when(edge & (n < DETOUR))
                 def _():
                     copy(
                         lbuf.at[INNER2, n], aside.at[n], ssem.at[S_ASIDE, 1], asidesem.at[n],
@@ -422,13 +452,18 @@
 
             late = n - 2
 
-            @pl.when((n >= 2) & (late - (late // LN) * LN < DETOUR) & jnp.logical_not(edge))
+            @pl.when((n < 2) & jnp.logical_not(edge))
+            def _():
+                onward_u(UN - 2 + n)
+
+            @pl.when((n >= 2) & (late < DETOUR) & jnp.logical_not(edge))
             def _():
                 onward(late)
 
             pl.when(n == 0)(tiles_0)
             pl.when(n == 1)(tiles_1)
             pl.when(n == 2)(tiles_2)
+            pl.when(n == 3)(tiles_3)
 
             @pl.when(n == NORM_STEP)
             def _():
@@ -540,19 +575,20 @@
 
     @pl.when(inner & jnp.logical_not(edge))
     def _():
-        some = aside.at[pl.ds(0, 2 * DETOUR)]
+        some = aside.at[pl.ds(0, DETOUR)]
         copy(some, some, ssem.at[S_ONWARD, 0], asidesem.at[0], sibling).wait_send()
+        copy(asideu, asideu, ssem.at[S_ONWARD, 1], asideusem.at[0], sibling).wait_send()
 
     @pl.when(edge & inner)
     def _():
         sent(OUTER2, S_WRAP_O)
         block = ubuf.at[INNER2]
-        copy(block, block, ssem.at[S_WRAP_I, 0], urecv.at[INNER2, 0], sibling).wait_send()
-        some = lbuf.at[INNER2, pl.ds(0, 2 * (LN - DETOUR))]
+        copy(block, block, ssem.at[S_ASIDE, 0], urecv.at[INNER2, 0], sibling).wait_send()
+        some = lbuf.at[INNER2, pl.ds(0, 2 * LN - DETOUR)]
         copy(some, some, ssem.at[S_WRAP_I, 1], lrecv.at[INNER2, 0], sibling).wait_send()
         row = norm.at[INNER2]
         copy(row, row, ssem.at[S_WRAP_I, 2], normrecv.at[INNER2], sibling).wait_send()
-        some = lbuf.at[INNER2, pl.ds(0, 2 * DETOUR)]
+        some = lbuf.at[INNER2, pl.ds(0, DETOUR)]
         copy(some, some, ssem.at[S_ASIDE, 1], lrecv.at[INNER2, 0], sibling).wait_send()
 
 
@@ -573,6 +609,7 @@
             pltpu.VMEM((LN, ROWS, LANE), F32),
             pltpu.VMEM((LN, ROWS, LANE), F32),
             part, part, part, part, half, half, half,
+            pltpu.VMEM((ROWS, WIDTH), BF16),
             pltpu.VMEM((SLOTS, 8, ROWS), F32),
             pltpu.SemaphoreType.DMA((15, 3)),
             pltpu.SemaphoreType.DMA((SLOTS, UN)),
@@ -581,6 +618,7 @@
             pltpu.SemaphoreType.DMA((2, 2 * LN)),
             pltpu.SemaphoreType.DMA((2 * LN,)),
             pltpu.SemaphoreType.DMA((2 * LN,)),
+            pltpu.SemaphoreType.DMA((UN,)),
             pltpu.SemaphoreType.DMA((SLOTS,)),
         ],
         compiler_params=pltpu.CompilerParams(

time: 134 us -> 130 us (0.970)
  Pallas kernels: 131 us -> 126 us
    pallas_call x1, Pallas kernels: 131 us -> 126 us  [body(): pl.pallas_call(kernel, out_shape=jax.ShapeDtypeStruct((ROWS, CLASSES), BF...]
where the time goes in v3:
time: 130 us; the launch traced here: 129 us
  Pallas kernels  126 us (97%)
  local copies, waits for them, and re-layouts  2 us (2%)
    pallas_call x1, Pallas kernels, body(): pl.pallas_call(kernel, out_shape=jax.ShapeDtypeStruct((ROWS, CLASSES), BF...  126 us

profile of v3, /device:TPU:1, one launch (start us, length us, event | category | flops | bytes accessed | tf_op | source)
XLA Modules:
  0.0 128.9 jit_solution(15793365785366893143)
XLA Ops:
  0.7 126.3 %shard_map.37 = bf16[384,896]{1,0:T(8,128)(2,1)} custom-call(s32[1]{0:T(128)S(6)} %copy.5.count_ref, bf16[384,768]{1,0:T(8,128)(2,1)} %emb_ref.1, bf16[384,896]{1,0:T(8,128)(2,1)} %lab_ref.1), custom_call_target="tpu_custom_call" | custom-call | flops 14000000000 | bytes 2000000 | tf_op jit(solution)/shard_map/pallas_call | solution.py:599
  126.9 2.0 %copy.6 = bf16[384,896]{1,0:T(8,128)(2,1)} copy(bf16[384,896]{1,0:T(8,128)(2,1)} %shard_map.37) | data formatting | bytes 1376256

commit v4 on v3

--- a/solution.py
+++ b/solution.py
@@ -350,11 +350,11 @@
 
         def combine(q, j):
             wait_part(precv1, 1, j)
-            ssend[j] = (acco[q] + precv1[j]).astype(BF16)
+            ssend[j] = (acco[q] + precv1[j].astype(F32)).astype(BF16)
 
             copy(ssend.at[j], srecv.at[j], ssem.at[S_SUM, 0], srsem.at[j], behind).start()
             wait_part(precv0, 0, j)
-            acc[q] += precv0[j]
+            acc[q] += precv0[j].astype(F32)
 
         def onward(j):
             copy(
@@ -380,14 +380,14 @@
                 product(T_OUTSIB, OWN, j)
                 + product(T_OUTSIB + 1, OUTER3, j)
                 + product(T_OUTSIB + 2, outsib_slot, j)
-            )
+            ).astype(BF16)
             send_part(psend1, precv1, 1, j)
             psend0[j] = (
                 product(T_SIB, OWN, j)
                 + product(T_SIB + 1, OUTER, j)
                 + product(T_SIB + 2, INNER2, j)
                 + product(T_SIB + 3, sib_slot, j)
-            )
+            ).astype(BF16)
             send_part(psend0, precv0, 0, j)
             acco[q] = (
                 product(T_OUT, OWN, j)
@@ -517,7 +517,7 @@
         def near(j, _):
             second = j // LN
             q = j - second * LN
-            psend0[j] = product(T_SIB, OWN, j)
+            psend0[j] = product(T_SIB, OWN, j).astype(BF16)
             send_part(psend0, precv0, 0, j)
             kept = jnp.where(second == 0, 0.0, 1.0 - keep_share)
             acc[q] = acc[q] * kept + product(T_OWN, OWN, j)
@@ -529,7 +529,7 @@
             wait_l(PREV, j)
             grouped = product(T_OWN + 5, NEXT, j) + product(T_OWN + 6, PREV, j)
             copy(srecv.at[j], srecv.at[j], ssem.at[S_SUM, 0], srsem.at[j], ahead).wait_recv()
-            acc[q] += precv0[j] + grouped + srecv[j].astype(F32)
+            acc[q] += precv0[j].astype(F32) + grouped + srecv[j].astype(F32)
             pl.when(j < LN)(lambda: send_sum(q))
 
         lax.fori_loop(0, LN, near, None)
@@ -594,7 +594,7 @@
 
 def body(embeddings, labels, cluster_rows):
     vmem = pl.BlockSpec(memory_space=pltpu.VMEM)
-    part = pltpu.VMEM((2 * LN, ROWS, LANE), F32)
+    part = pltpu.VMEM((2 * LN, ROWS, LANE), BF16)
     half = pltpu.VMEM((2 * LN, ROWS, LANE), BF16)
     return pl.pallas_call(
         kernel,

time: 130 us -> 130 us (level)
  no operation moved by 1% of the time
where the time goes in v4:
time: 130 us; the launch traced here: 128 us
  Pallas kernels  126 us (97%)
  local copies, waits for them, and re-layouts  2 us (2%)
    pallas_call x1, Pallas kernels, body(): pl.pallas_call(kernel, out_shape=jax.ShapeDtypeStruct((ROWS, CLASSES), BF...  126 us

profile of v4, /device:TPU:1, one launch (start us, length us, event | category | flops | bytes accessed | tf_op | source)
XLA Modules:
  0.0 128.3 jit_solution(4561624019028295360)
XLA Ops:
  0.7 125.7 %shard_map.37 = bf16[384,896]{1,0:T(8,128)(2,1)} custom-call(s32[1]{0:T(128)S(6)} %copy.5.count_ref, bf16[384,768]{1,0:T(8,128)(2,1)} %emb_ref.1, bf16[384,896]{1,0:T(8,128)(2,1)} %lab_ref.1), custom_call_target="tpu_custom_call" | custom-call | flops 14000000000 | bytes 2000000 | tf_op jit(solution)/shard_map/pallas_call | solution.py:599
  126.3 2.0 %copy.6 = bf16[384,896]{1,0:T(8,128)(2,1)} copy(bf16[384,896]{1,0:T(8,128)(2,1)} %shard_map.37) | data formatting | bytes 1376256
